TPU v7x, 32 devices: a whole 2x2x4 slice. The times are simulated.
32 devices in a mesh: band: 4 (over y, x), col: 8 (over z, core).
Axes of the slice: x: 2, y: 2, z: 4, core: 2. Of those that a mesh axis runs over, the one named last changes fastest.
Arguments:
- covariance: float32 [10240, 10240], P('col', 'band'), may hold values from -1 to 10, as said below
- wind_east: float32 [64, 160], replicated, may hold values from -0.25 to 0.25
- wind_north: float32 [64, 160], replicated, may hold values from -0.25 to 0.25
- obs_owner: int32 [3, 128], replicated, may hold values from 0 to 7, as said below
- obs_offset: int32 [3, 128], replicated, may hold values from 0 to 1279
- obs_variance: float32 [3, 128], replicated, may hold values from 0.3 to 3
Outputs:
- analysis: float32 [10240, 10240], P('col', 'band')
Inputs may be any that keep to these rules, and one draw needn't show every extreme that they name: `covariance`: symmetric positive definite. `obs_owner`: in every batch each slab index appears exactly 16 times.
All inputs are finite; a program needn't handle non-finite values.
Results may differ from a plain program's by a relative error of at most 0.00012.
Values sent between devices are 32-bit elements; how exact they have to be, the bound alone decides.
A program may use at most 128 MiB of HBM per device.

v0:
```python
import jax
import jax.numpy as jnp
from jax import lax
from jax.sharding import PartitionSpec as P


def extended(cells, sides, width):
    for axis, dim in sides:
        count = lax.axis_size(axis)
        ends = count - 1
        head = lax.slice_in_dim(cells, 0, width, axis=dim)
        tail = lax.slice_in_dim(cells, cells.shape[dim] - width, cells.shape[dim], axis=dim)
        cells = jnp.concatenate(
            [
                lax.ppermute(tail, axis, [(i, (i + 1) % count) for i in range(ends)]),
                cells,
                lax.ppermute(head, axis, [((i + 1) % count, i) for i in range(ends)]),
            ],
            axis=dim,
        )
    return cells


def advect(padded, east_wind, north_wind, lat_axis):
    length = padded.shape[lat_axis] - 2
    interior = lax.slice_in_dim(padded, 1, length + 1, axis=lat_axis)
    neighbour = jnp.roll(interior, -1, axis=lat_axis + 1)
    east_flux = jnp.maximum(east_wind, 0.0) * interior + jnp.minimum(east_wind, 0.0) * neighbour
    west_flux = jnp.roll(east_flux, 1, axis=lat_axis + 1)
    lower_cells = lax.slice_in_dim(padded, 0, length + 1, axis=lat_axis)
    upper_cells = lax.slice_in_dim(padded, 1, length + 2, axis=lat_axis)
    north_flux = (
        jnp.maximum(north_wind, 0.0) * lower_cells + jnp.minimum(north_wind, 0.0) * upper_cells
    )
    upper_flux = lax.slice_in_dim(north_flux, 1, length + 1, axis=lat_axis)
    lower_flux = lax.slice_in_dim(north_flux, 0, length, axis=lat_axis)
    return interior - (east_flux - west_flux) - (upper_flux - lower_flux)


def north_faces(wind_north):
    lat_count = wind_north.shape[0]
    lat_index = jnp.arange(lat_count)[:, None]
    walled = jnp.where(lat_index < lat_count - 1, wind_north, 0.0)
    return jnp.concatenate([jnp.zeros((1, wind_north.shape[1]), wind_north.dtype), walled], axis=0)


def solve_gain(matrix, right_side):
    factor = jnp.linalg.cholesky(matrix)
    middle = lax.linalg.triangular_solve(factor, right_side, left_side=True, lower=True)
    return lax.linalg.triangular_solve(factor, middle, left_side=True, lower=True, transpose_a=True)


def lead_product(gain_part, column_rows):
    return lax.dot_general(
        gain_part,
        column_rows,
        (((0,), (0,)), ((), ())),
        precision=lax.Precision.HIGHEST,
        preferred_element_type=jnp.float32,
    )


def local(covariance, wind_east, wind_north, obs_owner, obs_offset, obs_variance):
    slab_width, rows_local = covariance.shape
    longitude_count = wind_east.shape[1]
    strip_rows = rows_local // longitude_count
    slab_lat = slab_width // longitude_count
    col_count = lax.axis_size("col")
    band_id = lax.axis_index("band")
    col_id = lax.axis_index("col")
    face_winds = north_faces(wind_north)
    gridded = covariance.reshape(slab_width, strip_rows, longitude_count)
    padded = extended(gridded, (("band", 1),), 1)
    east_band = lax.dynamic_slice_in_dim(wind_east, band_id * strip_rows, strip_rows, 0)
    north_band = lax.dynamic_slice_in_dim(face_winds, band_id * strip_rows, strip_rows + 1, 0)
    advected = advect(padded, east_band[None], north_band[None], 1)
    flattened = advected.reshape(slab_lat, longitude_count, rows_local)
    grid_rim = extended(flattened, (("col", 0),), 1)
    east_slab = lax.dynamic_slice_in_dim(wind_east, col_id * slab_lat, slab_lat, 0)
    north_slab = lax.dynamic_slice_in_dim(face_winds, col_id * slab_lat, slab_lat + 1, 0)
    second_part = advect(grid_rim, east_slab[:, :, None], north_slab[:, :, None], 0)
    predicted_state = second_part.reshape(slab_width, rows_local)
    batch_count = obs_owner.shape[0]
    obs_count = obs_owner.shape[1]
    obs_slab = obs_count // col_count
    order_index = jnp.arange(obs_count)

    def arrange(batch_index):
        owners = obs_owner[batch_index]
        earlier = (owners[:, None] == owners[None, :]) & (
            order_index[None, :] < order_index[:, None]
        )
        places = owners * obs_slab + jnp.sum(earlier.astype(jnp.int32), axis=1)
        point_list = owners * slab_width + obs_offset[batch_index]
        ordered_points = jnp.zeros((obs_count,), jnp.int32).at[places].set(point_list)
        ordered_noise = (
            jnp.zeros((obs_count,), obs_variance.dtype).at[places].set(obs_variance[batch_index])
        )
        owned_rows = (
            lax.dynamic_slice_in_dim(ordered_points, col_id * obs_slab, obs_slab, 0)
            - col_id * slab_width
        )
        holders = ordered_points // rows_local
        index_local = jnp.clip(ordered_points - band_id * rows_local, 0, rows_local - 1)
        return (owned_rows, index_local, holders == band_id, ordered_noise)

    plans = [arrange(batch_index) for batch_index in range(batch_count)]
    for batch_index in range(batch_count):
        owned_rows, index_local, holder_flags, noise = plans[batch_index]
        column_rows = lax.all_gather(
            jnp.take(predicted_state, owned_rows, axis=0), "col", axis=0, tiled=True
        )
        chosen_rows = jnp.where(
            holder_flags[:, None], jnp.take(predicted_state, index_local, axis=1).T, 0.0
        )
        picked_block = jnp.where(
            holder_flags[:, None], jnp.take(column_rows, index_local, axis=1).T, 0.0
        )
        observation_rows, obs_block = lax.psum((chosen_rows, picked_block), "band")
        innovation = obs_block + jnp.diag(noise)
        weight_matrix = solve_gain(innovation, observation_rows)
        predicted_state = predicted_state - lead_product(weight_matrix, column_rows)
    return predicted_state


def solution(mesh):
    return jax.shard_map(
        local,
        mesh=mesh,
        in_specs=(P("col", "band"), P(), P(), P(), P(), P()),
        out_specs=P("col", "band"),
        check_vma=False,
    )
```

profile of v0, /device:TPU:0, one launch (start us, length us, event | category | flops | bytes accessed | tf_op | source)
XLA Modules:
  0.0 590.3 jit_solution(5356441808005894891)
XLA Ops:
  6.5 14.0 %copy.39 = f32[1280,2560]{0,1:T(8,128)} copy(f32[1280,2560]{1,0:T(8,128)} %param.17) | data formatting | bytes 26214400 | tf_op args[0]
  28.2 10.8 %slice.150 = f32[1280,16,159]{0,2,1:T(8,128)} slice(f32[1280,16,160]{0,2,1:T(8,128)} %bitcast.144), slice={[0:1280], [0:16], [1:160]} | slice | bytes 26050560 | tf_op jit(solution)/shard_map/jit(_roll_static)/slice | solution.py:27
  40.9 9.4 %fusion.4 = f32[1280,16,160]{0,2,1:T(8,128)S(1)} fusion(f32[1280,16,1]{0,2,1:T(1,128)S(1)} %slice.151, f32[1280,16,159]{0,2,1:T(8,128)} %slice.150, f32[1280,16,160]{0,2,1:T(8,128)} %bitcast.146, f32[16,160]{1,0:T(8,128)S(1)} %get-tuple-element.38, f32[16,160]{1,0:T(8,128)S(1)} %get-tuple-element.37), kind=kLoop, calls=%fused_computation.29 | loop fusion | flops 13107200 | bytes 39342080 | tf_op jit(solution)/shard_map/add | solution.py:28
  57.5 6.4 %collective-permute-done.1 = f32[1280,1,160]{0,2,1:T(8,128)} collective-permute-done((f32[1280,1,160]{0,2,1:T(8,128)S(1)}, f32[1280,1,160]{0,2,1:T(8,128)}, u32[]{:S(2)}, u32[]{:S(2)}) %collective-permute-start.1) | collective-permute-done | bytes 819232 | tf_op jit(solution)/shard_map/ppermute | solution.py:17
  63.9 15.0 %fusion.1 = f32[1280,17,160]{0,2,1:T(8,128)} fusion(f32[1280,16,160]{0,2,1:T(8,128)} %bitcast.147, f32[1280,1,160]{0,2,1:T(8,128)S(1)} %collective-permute-done, f32[1280,1,160]{0,2,1:T(8,128)} %collective-permute-done.1, f32[17,160]{1,0:T(8,128)S(1)} %get-tuple-element.40, f32[17,160]{1,0:T(8,128)S(1)} %get-tuple-element.39), kind=kLoop, calls=%fused_computation.22 | loop fusion | flops 17408000 | bytes 28693760 | tf_op jit(solution)/shard_map/add | solution.py:33
  81.4 18.6 %fusion.3 = f32[1280,16,160]{0,2,1:T(8,128)} fusion(f32[1280,17,160]{0,2,1:T(8,128)} %fusion.1, f32[1280,16,160]{0,2,1:T(8,128)} %bitcast.148, f32[1280,16,160]{0,2,1:T(8,128)S(1)} %bitcast.153, f32[1280,16,159]{0,2,1:T(8,128)S(1)} %bitcast.154, f32[1280,16,1]{0,2,1:T(1,128)S(1)} %slice.152), kind=kLoop, calls=%fused_computation.27 | loop fusion | flops 16384000 | bytes 78643200 | tf_op jit(solution)/shard_map/sub | solution.py:37
  114.0 20.6 %reshape.327 = f32[8,160,2560]{1,0,2:T(8,128)} reshape(f32[1280,16,160]{0,2,1:T(8,128)} %fusion.3) | data formatting | bytes 26214400 | tf_op jit(solution)/shard_map/reshape | solution.py:77
  134.6 18.4 %copy.57 = f32[8,160,2560]{2,1,0:T(8,128)} copy(f32[8,160,2560]{1,0,2:T(8,128)} %reshape.327) | data formatting | bytes 26214400 | tf_op jit(solution)/shard_map/reshape | solution.py:77
  152.9 11.3 %slice.158 = f32[8,159,2560]{2,1,0:T(8,128)} slice(f32[8,160,2560]{2,1,0:T(8,128)} %copy.57), slice={[0:8], [1:160], [0:2560]} | slice | bytes 26050560 | tf_op jit(solution)/shard_map/jit(_roll_static)/slice | solution.py:27
  165.4 11.0 %fusion.6 = f32[8,160,2560]{2,1,0:T(8,128)S(1)} fusion(f32[8,1,2560]{2,1,0:T(1,128)S(1)} %slice.159, f32[8,159,2560]{2,1,0:T(8,128)} %slice.158, f32[8,160,2560]{2,1,0:T(8,128)} %copy.57, f32[8,160]{1,0:T(8,128)S(1)} %get-tuple-element.34, f32[8,160]{1,0:T(8,128)S(1)} %get-tuple-element.33), kind=kLoop, calls=%fused_computation.33 | loop fusion | flops 13107200 | bytes 39331840 | tf_op jit(solution)/shard_map/add | solution.py:28
  178.3 7.5 %fusion = f32[9,160,2560]{2,1,0:T(8,128)} fusion(f32[8,160,2560]{2,1,0:T(8,128)S(1)} %copy-done, f32[1,160,2560]{2,1,0:T(8,128)} %collective-permute-done.2, f32[1,160,2560]{2,1,0:T(8,128)S(1)} %collective-permute-done.3, f32[9,160]{1,0:T(8,128)S(1)} %get-tuple-element.36, f32[9,160]{1,0:T(8,128)S(1)} %get-tuple-element.35), kind=kLoop, calls=%fused_computation.16 | loop fusion | flops 18432000 | bytes 31141120 | tf_op jit(solution)/shard_map/add | solution.py:33
  186.1 25.0 %fusion.2 = f32[8,160,2560]{2,1,0:T(8,128)} fusion(f32[9,160,2560]{2,1,0:T(8,128)} %fusion, f32[8,160,2560]{2,1,0:T(8,128)S(1)} %copy-done, f32[8,160,2560]{2,1,0:T(8,128)} %copy-done.2, f32[8,159,2560]{2,1,0:T(8,128)} %bitcast.155, f32[8,1,2560]{2,1,0:T(1,128)S(1)} %slice.160), kind=kLoop, calls=%fused_computation.25 | loop fusion | flops 16384000 | bytes 78643200 | tf_op jit(solution)/shard_map/sub | solution.py:37
  211.0 5.4 gather_fusion
  217.3 14.0 %copy.47 = f32[1280,2560]{0,1:T(8,128)} copy(f32[1280,2560]{1,0:T(8,128)} %bitcast.150) | data formatting | bytes 26214400 | tf_op jit(solution)/shard_map/reshape | solution.py:82
  231.3 6.0 %gather_fusion.2 = f32[128,1280]{1,0:T(8,128)S(1)} fusion(f32[1280,2560]{0,1:T(8,128)} %copy.47, s32[1024]{0:T(1024)S(1)} %pad_clamp_fusion.4), kind=kCustom, calls=%fused_computation.2.clone | custom fusion | bytes 1311232 | tf_op jit(solution)/shard_map/jit(_take)/gather | solution.py:114
  248.3 45.3 %all-reduce.12.cloned.1.call-done = (f32[128,1280]{1,0:T(8,128)}, f32[128,128]{0,1:T(8,128)}) async-done(((f32[128,1280]{1,0:T(8,128)}, f32[128,128]{0,1:T(8,128)}), (f32[128,1280]{1,0:T(8,128)}, f32[128,128]{0,1:T(8,128)})) %all-reduce.12.cloned.1.call-update) | async-done | bytes 720912 | tf_op jit(solution)/shard_map/psum | solution.py:119
  295.5 11.7 %cholesky.59 = f32[128,128]{1,0:T(8,128)S(1)} custom-call(f32[128,128]{1,0:T(8,128)S(1)} %fusion.30), custom_call_target="Cholesky" | custom-call | tf_op jit(solution)/shard_map/jit(cholesky)/cholesky | solution.py:48
  308.6 9.8 %custom-call.13 = f32[1,128,128]{1,2,0:T(8,128)S(1)} custom-call(f32[1,128,128]{2,1,0:T(8,128)S(1)} %fusion.11), custom_call_target="InvertDiagBlocksLowerTriangular" | custom-call | tf_op jit(solution)/shard_map/triangular_solve/custom-call.2 | solution.py:50
  320.9 15.8 %convolution_subtract_fusion.2 = f32[1280,2560]{1,0:T(8,128)} fusion(f32[1280,2560]{1,0:T(8,128)} %bitcast.151, f32[128,1280]{1,0:T(8,128)S(1)} %fusion.28, f32[128,2560]{1,0:T(8,128)} %all-gather.4.cloned.1.call-done), kind=kOutput, calls=%fused_computation.20 | convolution fusion | flops 5036441600 | bytes 28180480 | tf_op jit(solution)/shard_map/dot_general | solution.py:54
  336.7 5.4 gather_fusion.3
  342.9 14.0 %copy.52 = f32[1280,2560]{0,1:T(8,128)} copy(f32[1280,2560]{1,0:T(8,128)} %convolution_subtract_fusion.2) | data formatting | bytes 26214400 | tf_op jit(solution)/shard_map/sub | solution.py:122
  356.9 6.0 %gather_fusion.5 = f32[128,1280]{1,0:T(8,128)S(1)} fusion(f32[1280,2560]{0,1:T(8,128)} %copy.52, s32[1024]{0:T(1024)S(1)} %pad_clamp_fusion.2), kind=kCustom, calls=%fused_computation.7.clone | custom fusion | bytes 1311232 | tf_op jit(solution)/shard_map/jit(_take)/gather | solution.py:114
  371.9 45.3 %all-reduce.10.cloned.1.call-done = (f32[128,1280]{1,0:T(8,128)}, f32[128,128]{0,1:T(8,128)}) async-done(((f32[128,1280]{1,0:T(8,128)}, f32[128,128]{0,1:T(8,128)}), (f32[128,1280]{1,0:T(8,128)}, f32[128,128]{0,1:T(8,128)})) %all-reduce.10.cloned.1.call-update) | async-done | bytes 720912 | tf_op jit(solution)/shard_map/psum | solution.py:119
  419.0 11.7 %cholesky.70 = f32[128,128]{1,0:T(8,128)S(1)} custom-call(f32[128,128]{1,0:T(8,128)S(1)} %fusion.24), custom_call_target="Cholesky" | custom-call | tf_op jit(solution)/shard_map/jit(cholesky)/cholesky | solution.py:48
  432.1 9.8 %custom-call.15 = f32[1,128,128]{1,2,0:T(8,128)S(1)} custom-call(f32[1,128,128]{2,1,0:T(8,128)S(1)} %fusion.12), custom_call_target="InvertDiagBlocksLowerTriangular" | custom-call | tf_op jit(solution)/shard_map/triangular_solve/custom-call.2 | solution.py:50
  444.4 15.8 %convolution_subtract_fusion.1 = f32[1280,2560]{1,0:T(8,128)} fusion(f32[1280,2560]{1,0:T(8,128)} %convolution_subtract_fusion.2, f32[128,1280]{1,0:T(8,128)S(1)} %fusion.22, f32[128,2560]{1,0:T(8,128)} %all-gather.6.cloned.1.call-done), kind=kOutput, calls=%fused_computation.19 | convolution fusion | flops 5036441600 | bytes 28180480 | tf_op jit(solution)/shard_map/dot_general | solution.py:54
  466.7 14.0 %copy.56 = f32[1280,2560]{0,1:T(8,128)} copy(f32[1280,2560]{1,0:T(8,128)} %convolution_subtract_fusion.1) | data formatting | bytes 26214400 | tf_op jit(solution)/shard_map/sub | solution.py:122
  480.7 6.0 %gather_fusion.8 = f32[128,1280]{1,0:T(8,128)S(1)} fusion(f32[1280,2560]{0,1:T(8,128)} %copy.56, s32[1024]{0:T(1024)S(1)} %pad_clamp_fusion), kind=kCustom, calls=%fused_computation.8.clone | custom fusion | bytes 1311232 | tf_op jit(solution)/shard_map/jit(_take)/gather | solution.py:114
  494.1 46.7 %all-reduce.8.cloned.1.call-done = (f32[128,1280]{1,0:T(8,128)}, f32[128,128]{1,0:T(8,128)}) async-done(((f32[128,1280]{1,0:T(8,128)}, f32[128,128]{1,0:T(8,128)}), (f32[128,1280]{1,0:T(8,128)}, f32[128,128]{1,0:T(8,128)})) %all-reduce.8.cloned.1.call-update) | async-done | bytes 720912 | tf_op jit(solution)/shard_map/psum | solution.py:119
  541.8 11.7 %cholesky.81 = f32[128,128]{1,0:T(8,128)S(1)} custom-call(f32[128,128]{1,0:T(8,128)S(1)} %fusion.18), custom_call_target="Cholesky" | custom-call | tf_op jit(solution)/shard_map/jit(cholesky)/cholesky | solution.py:48
  554.9 9.8 %custom-call.17 = f32[1,128,128]{1,2,0:T(8,128)S(1)} custom-call(f32[1,128,128]{2,1,0:T(8,128)S(1)} %fusion.13), custom_call_target="InvertDiagBlocksLowerTriangular" | custom-call | tf_op jit(solution)/shard_map/triangular_solve/custom-call.2 | solution.py:50
  567.2 15.8 %convolution_subtract_fusion = f32[1280,2560]{1,0:T(8,128)} fusion(f32[1280,2560]{1,0:T(8,128)} %convolution_subtract_fusion.1, f32[128,1280]{1,0:T(8,128)S(1)} %fusion.16, f32[128,2560]{1,0:T(8,128)} %all-gather.8.cloned.1.call-done), kind=kOutput, calls=%fused_computation.18 | convolution fusion | flops 5036441600 | bytes 28180480 | tf_op jit(solution)/shard_map/dot_general | solution.py:54
  (126 shorter events, 87.9 us)
Async XLA Ops:
  6.5 236.4 %all-gather.4.cloned.1.call-start = ((), (), s32[]{:S(2)}) async-start(), calls=%async_computation | async-start | bytes 1474560 | tf_op jit(solution)/shard_map/all_gather | solution.py:110
  22.0 35.5 %collective-permute-start = (f32[1280,1,160]{0,2,1:T(8,128)S(1)}, f32[1280,1,160]{0,2,1:T(8,128)S(1)}, u32[]{:S(2)}, u32[]{:S(2)}) collective-permute-start(f32[1280,1,160]{0,2,1:T(8,128)S(1)} %get-tuple-element.32), channel_id=1, source_target_pairs={{0,8},{8,16},{16,24},{1,9},{9,17},{17,25},{2,10},{10,18},{18,26},{... | collective-permute-start | bytes 2457608 | tf_op jit(solution)/shard_map/ppermute | solution.py:15
  26.9 37.0 %collective-permute-start.1 = (f32[1280,1,160]{0,2,1:T(8,128)S(1)}, f32[1280,1,160]{0,2,1:T(8,128)}, u32[]{:S(2)}, u32[]{:S(2)}) collective-permute-start(f32[1280,1,160]{0,2,1:T(8,128)S(1)} %get-tuple-element.31), channel_id=1, source_target_pairs={{8,0},{16,8},{24,16},{9,1},{17,9},{25,17},{10,2},{18,10},{26,18},{... | collective-permute-start | bytes 2457608 | tf_op jit(solution)/shard_map/ppermute | solution.py:17
  40.9 14.3 %copy-start.4 = (s32[3,128]{1,0:T(4,128)S(1)}, s32[3,128]{1,0:T(4,128)}, u32[]{:S(2)}) copy-start(s32[3,128]{1,0:T(4,128)} %param.20) | copy-start | bytes 4612
  40.9 14.5 %copy-start.6 = (s32[3,128]{1,0:T(4,128)S(1)}, s32[3,128]{1,0:T(4,128)}, u32[]{:S(2)}) copy-start(s32[3,128]{1,0:T(4,128)} %param.21) | copy-start | bytes 4612
  40.9 16.5 %copy-start.3 = (f32[64,160]{1,0:T(8,128)S(1)}, f32[64,160]{1,0:T(8,128)}, u32[]{:S(2)}) copy-start(f32[64,160]{1,0:T(8,128)} %param.19) | copy-start | bytes 122884
  50.3 4.8 copy-start.1
  55.6 23.3 %slice-start = ((s8[13107200]{0:T(1024)(128)(4,1)}), s8[524288]{0:T(1024)(128)(4,1)S(1)}, s32[]{:S(2)}) async-start(s8[13107200]{0:T(1024)(128)(4,1)} %bitcast.152), calls=%async_computation.6 | async-start | bytes 1048576
  63.9 15.0 %slice-start.1 = ((s8[13107200]{0:T(1024)(128)(4,1)}), s8[4194304]{0:T(1024)(128)(4,1)S(1)}, s32[]{:S(2)}) async-start(s8[13107200]{0:T(1024)(128)(4,1)} %bitcast.152), calls=%async_computation.7 | async-start | bytes 8388608
  63.9 16.3 %slice-start.2 = ((s8[13107200]{0:T(1024)(128)(4,1)}), s8[4194304]{0:T(1024)(128)(4,1)S(1)}, s32[]{:S(2)}) async-start(s8[13107200]{0:T(1024)(128)(4,1)} %bitcast.152), calls=%async_computation.8 | async-start | bytes 8388608
  63.9 17.4 %slice-start.3 = ((s8[13107200]{0:T(1024)(128)(4,1)}), s8[4194304]{0:T(1024)(128)(4,1)S(1)}, s32[]{:S(2)}) async-start(s8[13107200]{0:T(1024)(128)(4,1)} %bitcast.152), calls=%async_computation.9 | async-start | bytes 8388608
  107.9 68.6 %collective-permute-start.2 = (f32[1,160,2560]{2,1,0:T(8,128)}, f32[1,160,2560]{2,1,0:T(8,128)}, u32[]{:S(2)}, u32[]{:S(2)}) collective-permute-start(f32[1,160,2560]{2,1,0:T(8,128)} %copy.41), channel_id=1, source_target_pairs={{0,1},{1,2},{2,3},{3,4},{4,5},{5,6},{6,7},{8,9},{9,10},{10,11},{11... | collective-permute-start | bytes 4915208 | tf_op jit(solution)/shard_map/ppermute | solution.py:15
  112.2 64.3 %collective-permute-start.3 = (f32[1,160,2560]{2,1,0:T(8,128)}, f32[1,160,2560]{2,1,0:T(8,128)S(1)}, u32[]{:S(2)}, u32[]{:S(2)}) collective-permute-start(f32[1,160,2560]{2,1,0:T(8,128)} %copy.42), channel_id=1, source_target_pairs={{1,0},{2,1},{3,2},{4,3},{5,4},{6,5},{7,6},{9,8},{10,9},{11,10},{12... | collective-permute-start | bytes 4915208 | tf_op jit(solution)/shard_map/ppermute | solution.py:17
  165.3 12.9 %copy-start = (f32[8,160,2560]{2,1,0:T(8,128)S(1)}, f32[8,160,2560]{2,1,0:T(8,128)}, u32[]{:S(2)}) copy-start(f32[8,160,2560]{2,1,0:T(8,128)} %copy.57) | copy-start | bytes 39321604
  176.4 9.7 %copy-start.2 = (f32[8,160,2560]{2,1,0:T(8,128)}, f32[8,160,2560]{2,1,0:T(8,128)S(1)}, u32[]{:S(2)}) copy-start(f32[8,160,2560]{2,1,0:T(8,128)S(1)} %fusion.6) | copy-start | bytes 39321604
  217.2 76.4 %all-reduce.12.cloned.1.call-start = ((), (), s32[]{:S(2)}) async-start(), calls=%async_computation.5 | async-start | bytes 1441792 | tf_op jit(solution)/shard_map/psum | solution.py:119
  217.3 28.8 %copy-start.5 = (f32[3,128]{1,0:T(4,128)S(1)}, f32[3,128]{1,0:T(4,128)}, u32[]{:S(2)}) copy-start(f32[3,128]{1,0:T(4,128)} %param.22) | copy-start | bytes 4612
  246.0 120.4 %all-gather.6.cloned.1.call-start = ((), (), s32[]{:S(2)}) async-start(), calls=%async_computation.1 | async-start | bytes 1474560 | tf_op jit(solution)/shard_map/all_gather | solution.py:110
  342.9 74.3 %all-reduce.10.cloned.1.call-start = ((), (), s32[]{:S(2)}) async-start(), calls=%async_computation.4 | async-start | bytes 1441792 | tf_op jit(solution)/shard_map/psum | solution.py:119
  369.6 120.4 %all-gather.8.cloned.1.call-start = ((), (), s32[]{:S(2)}) async-start(), calls=%async_computation.2 | async-start | bytes 1474560 | tf_op jit(solution)/shard_map/all_gather | solution.py:110
  466.4 74.3 %all-reduce.8.cloned.1.call-start = ((), (), s32[]{:S(2)}) async-start(), calls=%async_computation.3 | async-start | bytes 1441792 | tf_op jit(solution)/shard_map/psum | solution.py:119
Sparse Core Ops, SparseCore 0:
  217.3 25.5 all-gather.3
  246.1 47.4 all-reduce.11
  343.0 23.4 all-gather.5
  369.7 47.4 all-reduce.9
  466.5 23.4 all-gather.7
  493.2 47.4 all-reduce.7
where the time goes:
time: 599 us; the launch traced here: 590 us
  local copies, waits for them, and re-layouts  189 us (32%)
  other arithmetic  168 us (28%)
  waiting for transfers between devices  153 us (26%)
  matrix products  54.9 us (9%)
  between operations  14.5 us (2%)
  starting transfers between devices  10.9 us (2%)
    psum x3, waiting for transfers between devices, local(): observation_rows, obs_block = lax.psum((chosen_rows, picked_block), 'band')  137 us
    dot_general x3, matrix products, lead_product(): lax.dot_general(gain_part, column_rows, (((0,), (0,)), ((), ())), precisi...  47.5 us
    sub x2, other arithmetic, advect(): return interior - (east_flux - west_flux) - (upper_flux - lower_flux)  43.6 us
    reshape x2, local copies, waits for them, and re-layouts, local(): flattened = advected.reshape(slab_lat, longitude_count, rows_local)  38.9 us
    another operation x9, other arithmetic, solve_gain(): factor = jnp.linalg.cholesky(matrix)  37.3 us
    another operation x6, other arithmetic, solve_gain(): lax.linalg.triangular_solve(factor, middle, left_side=True, lower=True, t...  31.3 us
    sub x2, local copies, waits for them, and re-layouts, local(): predicted_state = predicted_state - lead_product(weight_matrix, column_rows)  28 us
    slice x4, local copies, waits for them, and re-layouts, advect(): neighbour = jnp.roll(interior, -1, axis=lat_axis + 1)  24.4 us
  transfers between devices with their start and end apart: 10, of which 7 were waited for; matrix products, arithmetic and copies ran while one was open for 27% of the time, Pallas kernels for 0%

commit v1 on v0

v1 whole, which is shorter than its diff:
```python
import functools

import jax
import jax.numpy as jnp
from jax import lax
from jax.experimental import pallas as pl
from jax.experimental.pallas import tpu as pltpu
from jax.sharding import PartitionSpec as P

LANES = 128
SUBLANES = 8
PIVOT = 128
VMEM_BYTES = 56 * 1024 * 1024
HIGHEST = lax.Precision.HIGHEST


def stencil_weights(wind_east, wind_north):
    walls = jnp.concatenate([jnp.zeros((1, wind_north.shape[1]), wind_north.dtype), wind_north[:-1], jnp.zeros((1, wind_north.shape[1]), wind_north.dtype)], axis=0)
    west_wind = jnp.roll(wind_east, 1, axis=1)
    upper, lower = walls[1:], walls[:-1]
    own = (
        1.0
        - (jnp.maximum(wind_east, 0.0) - jnp.minimum(west_wind, 0.0))
        - (jnp.maximum(upper, 0.0) - jnp.minimum(lower, 0.0))
    )
    return jnp.stack(
        [own, -jnp.minimum(wind_east, 0.0), jnp.maximum(west_wind, 0.0), -jnp.minimum(upper, 0.0), jnp.maximum(lower, 0.0)]
    )


def lane_weights(weights, lon, strip):
    own, east, west, north, south = weights.reshape(5, -1)
    place = jnp.arange(own.shape[0]) % lon
    first, last = place == 0, place == lon - 1
    here = lambda w: jnp.pad(w, (strip, strip))
    above = lambda w: jnp.pad(w, (strip + lon, strip - lon))
    below = lambda w: jnp.pad(w, (strip - lon, strip + lon))
    rows = [
        here(own),
        here(jnp.where(last, 0.0, east)),
        here(jnp.where(first, 0.0, west)),
        above(north),
        above(jnp.where(first, west, 0.0)),
        below(south),
        below(jnp.where(last, east, 0.0)),
    ]
    return jnp.stack(rows + [jnp.zeros_like(rows[0])])


def along_lanes(cells, lane_ref, lon, strip):
    width = cells.shape[1]
    weight = lambda k: lane_ref[k : k + 1, :]
    east = pltpu.roll(cells, width - 1, 1)
    west = pltpu.roll(cells, 1, 1)
    north = weight(3) * cells + weight(4) * west
    south = weight(5) * cells + weight(6) * east
    total = weight(0) * cells + weight(1) * east + weight(2) * west
    total += pltpu.roll(north, width - lon, 1) + pltpu.roll(south, lon, 1)
    return total[:, strip : width - strip]


def rim_copies(refs, ext_ref, sems, lon, strip):
    cov, left, right, top, bottom, top_ends, bottom_ends = refs
    rows, band = cov.shape
    mid, cols = pl.ds(lon, rows), pl.ds(strip, band)
    ends = (pl.ds(0, strip), pl.ds(strip + band, strip))
    high = pl.ds(lon + rows, lon)
    pairs = [
        (left, ext_ref.at[mid, ends[0]]),
        (right, ext_ref.at[mid, ends[1]]),
        (top, ext_ref.at[pl.ds(0, lon), cols]),
        (bottom, ext_ref.at[high, cols]),
    ]
    for side in range(2):
        part = pl.ds(side * strip, strip)
        pairs.append((top_ends.at[:, part], ext_ref.at[pl.ds(0, lon), ends[side]]))
        pairs.append((bottom_ends.at[:, part], ext_ref.at[high, ends[side]]))
    return [pltpu.make_async_copy(src, dst, sems.at[k]) for k, (src, dst) in enumerate(pairs)]


def block_copy(cov, ext_ref, sems, lon, strip, step):
    rows = pl.ds(pl.multiple_of(step * lon, SUBLANES), lon)
    dst = pl.ds(pl.multiple_of((step + 1) * lon, SUBLANES), lon)
    return pltpu.make_async_copy(cov.at[rows, :], ext_ref.at[dst, pl.ds(strip, cov.shape[1])], sems.at[step])


def observed_kernel(lon, strip, count, spots, row_weights, lanes, *rest):
    refs, (out, ext, picked, rim_sems, block_sems) = rest[:7], rest[7:]
    rows = refs[0].shape[0]
    steps = rows // lon
    copies = rim_copies(refs, ext, rim_sems, lon, strip)
    for step in range(steps):
        block_copy(refs[0], ext, block_sems, lon, strip, step).start()
    for copy in copies:
        copy.start()
    picked[...] = jnp.zeros_like(picked)
    for step in range(steps):
        block_copy(refs[0], ext, block_sems, lon, strip, step).wait()
    for copy in copies:
        copy.wait()

    @pl.loop(0, count)
    def _(k):
        spot = spots[k]
        place = lax.rem(spot, lon)
        east = jnp.where(place == lon - 1, spot + 1 - lon, spot + 1)
        west = jnp.where(place == 0, spot + lon - 1, spot - 1)
        total = row_weights[spot] * ext[pl.ds(lon + spot, 1), :]
        for which, row in enumerate((lon + east, lon + west, 2 * lon + spot, spot)):
            total += row_weights[(which + 1) * rows + spot] * ext[pl.ds(row, 1), :]
        picked[pl.ds(k, 1), :] = total

    for group in range(picked.shape[0] // SUBLANES):
        part = pl.ds(group * SUBLANES, SUBLANES)
        out[part, :] = along_lanes(picked[part, :], lanes, lon, strip)


def forecast_kernel(lon, strip, row_weights, lanes, *rest):
    refs, (out, ext, rim_sems, block_sems) = rest[:7], rest[7:]
    steps = refs[0].shape[0] // lon
    step = pl.program_id(0)
    groups = lon // SUBLANES
    copies = rim_copies(refs, ext, rim_sems, lon, strip)
    fetch = functools.partial(block_copy, refs[0], ext, block_sems, lon, strip)

    @pl.when(step == 0)
    def _():
        for copy in copies:
            copy.start()
        for s in range(steps):
            fetch(s).start()
        for copy in copies:
            copy.wait()
        fetch(0).wait()

    @pl.when(step + 1 < steps)
    def _():
        fetch(step + 1).wait()

    base = (step + 1) * lon
    line = lax.broadcasted_iota(jnp.int32, (SUBLANES, ext.shape[1]), 0)
    read = lambda row: ext[pl.ds(pl.multiple_of(row, SUBLANES), SUBLANES), :]

    @pl.loop(0, groups)
    def _(group):
        row = base + group * SUBLANES
        after = base + jnp.where(group == groups - 1, 0, group + 1) * SUBLANES
        before = base + jnp.where(group == 0, groups - 1, group - 1) * SUBLANES
        cells = read(row)
        east = jnp.where(line == SUBLANES - 1, pltpu.roll(read(after), SUBLANES - 1, 0), pltpu.roll(cells, SUBLANES - 1, 0))
        west = jnp.where(line == 0, pltpu.roll(read(before), 1, 0), pltpu.roll(cells, 1, 0))
        part = pl.ds(pl.multiple_of(group * SUBLANES, SUBLANES), SUBLANES)
        factors = row_weights[part, :]
        factor = lambda k: factors[:, k : k + 1]
        total = factor(0) * cells + factor(1) * east + factor(2) * west
        total += factor(3) * read(row + lon) + factor(4) * read(row - lon)
        out[part, :] = along_lanes(total, lanes, lon, strip)


def spread(block, k):
    return jnp.take_along_axis(block, jnp.full(block.shape, k, jnp.int32), axis=1, mode="promise_in_bounds")


def inverse_kernel(source, out, work):
    size = source.shape[0]
    out[...] = source[...]
    sub = lax.broadcasted_iota(jnp.int32, (PIVOT, PIVOT), 0)
    lane = lax.broadcasted_iota(jnp.int32, (PIVOT, PIVOT), 1)
    dot = functools.partial(jnp.dot, precision=HIGHEST, preferred_element_type=jnp.float32)
    for at in range(0, size, PIVOT):
        mine = pl.ds(at, PIVOT)
        work[...] = out[mine, mine]

        def pivot(k, carry):
            block = work[...]
            row = work[pl.ds(k, 1), :]
            column = spread(block, k)
            scale = 1.0 / spread(jnp.broadcast_to(row, (SUBLANES, PIVOT)), k)[:1]
            scaled = row * scale
            on_row, on_lane = sub == k, lane == k
            rest = block - column * scaled
            rest = jnp.where(on_lane, -column * scale, rest)
            work[...] = jnp.where(on_row, jnp.where(on_lane, scale, scaled), rest)
            return carry

        lax.fori_loop(0, PIVOT, pivot, 0)
        inverse = work[...]
        column = out[:, mine]
        row = dot(inverse, out[mine, :])
        out[...] = out[...] - dot(column, row)
        out[:, mine] = -dot(column, inverse)
        out[mine, :] = row
        out[mine, mine] = inverse


def local(covariance, wind_east, wind_north, obs_owner, obs_offset, obs_variance):
    slab, band = covariance.shape
    lat, lon = wind_east.shape
    strip = -(-lon // LANES) * LANES
    strip_rows, slab_rows = band // lon, slab // lon
    col_count, band_count = lax.axis_size("col"), lax.axis_size("band")
    band_id, col_id = lax.axis_index("band"), lax.axis_index("col")

    onward = lambda x, axis, n: lax.ppermute(x, axis, [(i, i + 1) for i in range(n - 1)])
    back = lambda x, axis, n: lax.ppermute(x, axis, [(i + 1, i) for i in range(n - 1)])
    left = onward(covariance[:, band - strip :], "band", band_count)
    right = back(covariance[:, :strip], "band", band_count)
    top = onward(covariance[slab - lon :, :], "col", col_count)
    bottom = back(covariance[:lon, :], "col", col_count)
    ends = lambda rows: jnp.concatenate([left[rows], right[rows]], axis=1)
    top_ends = onward(ends(slice(slab - lon, slab)), "col", col_count)
    bottom_ends = back(ends(slice(0, lon)), "col", col_count)
    rims = (covariance, left, right, top, bottom, top_ends, bottom_ends)

    weights = stencil_weights(wind_east, wind_north)
    lanes = lane_weights(lax.dynamic_slice_in_dim(weights, band_id * strip_rows, strip_rows, 1), lon, strip)
    row_weights = lax.dynamic_slice_in_dim(weights, col_id * slab_rows, slab_rows, 1).reshape(5, slab)

    obs_total = obs_owner.size
    own_count = obs_total // col_count
    owners = obs_owner.reshape(-1)
    order = jnp.arange(obs_total)
    earlier = (owners[:, None] == owners[None, :]) & (order[None, :] < order[:, None])
    places = owners * own_count + jnp.sum(earlier.astype(jnp.int32), axis=1)
    hit = places[None, :] == order[:, None]
    offsets = jnp.sum(jnp.where(hit, obs_offset.reshape(1, -1), 0), axis=1)
    noise = jnp.sum(jnp.where(hit, obs_variance.reshape(1, -1), 0.0), axis=1)
    spots = lax.dynamic_slice_in_dim(offsets, col_id * own_count, own_count, 0)

    ext_shape = pltpu.VMEM((slab + 2 * lon, band + 2 * strip), jnp.float32)
    sems = [pltpu.SemaphoreType.DMA((8,)), pltpu.SemaphoreType.DMA((slab_rows,))]
    anywhere = [pl.BlockSpec(memory_space=pl.ANY)] * 7
    in_smem = pl.BlockSpec(memory_space=pltpu.SMEM)
    in_vmem = pl.BlockSpec(memory_space=pltpu.VMEM)
    params = pltpu.CompilerParams(vmem_limit_bytes=VMEM_BYTES)
    padded = -(-own_count // SUBLANES) * SUBLANES
    observed = pl.pallas_call(
        functools.partial(observed_kernel, lon, strip, own_count),
        out_shape=jax.ShapeDtypeStruct((padded, band), jnp.float32),
        in_specs=[in_smem, in_smem, in_vmem] + anywhere,
        out_specs=in_vmem,
        scratch_shapes=[ext_shape, pltpu.VMEM((padded, band + 2 * strip), jnp.float32)] + sems,
        compiler_params=params,
        cost_estimate=pl.CostEstimate(flops=10**7, bytes_accessed=4 * slab * band, transcendentals=0),
    )(spots, row_weights.reshape(-1), lanes, *rims)[:own_count]

    forecast = pl.pallas_call(
        functools.partial(forecast_kernel, lon, strip),
        grid=(slab_rows,),
        out_shape=jax.ShapeDtypeStruct((slab, band), jnp.float32),
        in_specs=[pl.BlockSpec((lon, 8), lambda s: (s, 0)), pl.BlockSpec((8, band + 2 * strip), lambda s: (0, 0))] + anywhere,
        out_specs=pl.BlockSpec((lon, band), lambda s: (s, 0)),
        scratch_shapes=[ext_shape] + sems,
        compiler_params=params,
        cost_estimate=pl.CostEstimate(flops=30 * slab * band, bytes_accessed=32 * slab * band, transcendentals=0),
    )(jnp.pad(row_weights, ((0, 3), (0, 0))).T, lanes, *rims)

    band_rows = lax.all_gather(observed, "col", axis=0, tiled=True)
    pieces = observed.reshape(own_count, band // slab, slab).transpose(1, 0, 2)
    pieces = lax.all_gather(pieces, "band", axis=0, tiled=True)
    slab_part = lax.all_to_all(pieces, "col", 0, 0, tiled=True).reshape(obs_total, slab)
    chosen = (spots[:, None] == jnp.arange(slab)[None, :]).astype(jnp.float32)
    own_block = lax.dot_general(chosen, slab_part, (((1,), (1,)), ((), ())), precision=HIGHEST, preferred_element_type=jnp.float32)
    innovation = lax.all_gather(own_block, "col", axis=0, tiled=True)
    innovation = jnp.where(order[:, None] == order[None, :], innovation + noise[:, None], innovation)

    inverse = pl.pallas_call(
        inverse_kernel,
        out_shape=jax.ShapeDtypeStruct(innovation.shape, jnp.float32),
        in_specs=[in_vmem],
        out_specs=in_vmem,
        scratch_shapes=[pltpu.VMEM((PIVOT, PIVOT), jnp.float32)],
        compiler_params=params,
    )(innovation)
    gain = jnp.dot(inverse, slab_part, precision=HIGHEST, preferred_element_type=jnp.float32)
    change = lax.dot_general(gain, band_rows, (((0,), (0,)), ((), ())), precision=lax.Precision.HIGH, preferred_element_type=jnp.float32)
    return forecast - change


def solution(mesh):
    return jax.shard_map(
        local,
        mesh=mesh,
        in_specs=(P("col", "band"), P(), P(), P(), P(), P()),
        out_specs=P("col", "band"),
        check_vma=False,
    )
```

time: 599 us -> 314 us (0.52); the launches traced: 590 us -> 313 us
  local copies, waits for them, and re-layouts: 189 us -> 14 us
  other arithmetic: 168 us -> 14.5 us
  Pallas kernels: 0 us -> 107 us
  waiting for transfers between devices: 153 us -> 108 us
  matrix products: 54.9 us -> 21 us
  blocking collectives: 0 us -> 15.2 us
  starting transfers between devices: 10.9 us -> 19.8 us
    psum x3 -> x0, waiting for transfers between devices: 137 us -> none  [local(): observation_rows, obs_block = lax.psum((chosen_rows, picked_block), 'band')]
    pallas_call x0 -> x3, Pallas kernels: none -> 107 us  [the longest x1 54.1 us: local(): pl.pallas_call(functools.partial(forecast_kernel, lon, strip), grid=(slab...]
    another operation x15 -> x1, other arithmetic: 68.6 us -> 0.01 us  [stencil_weights(): jnp.stack([own, -jnp.minimum(wind_east, 0.0), jnp.maximum(west_wind, 0.0)...]
    all_gather x3 -> x2, waiting for transfers between devices: 9.39 us -> 65.4 us  [the longest x1 65.4 us: local(): pieces = lax.all_gather(pieces, 'band', axis=0, tiled=True)]
    reshape x3 -> x1, local copies, waits for them, and re-layouts: 52.9 us -> 1.84 us  [local(): pieces = observed.reshape(own_count, band // slab, slab).transpose(1, 0, 2)]
    add x8 -> x1, other arithmetic: 44.7 us -> 0.01 us  [local(): places = owners * own_count + jnp.sum(earlier.astype(jnp.int32), axis=1)]
    gather x11 -> x0, local copies, waits for them, and re-layouts: 36.2 us -> none  [the longest x3 17.9 us: local(): jnp.take(predicted_state, index_local, axis=1)]
    sub x2 -> x1, other arithmetic: 43.6 us -> 11.1 us  [local(): return forecast - change]
  transfers between devices with their start and end apart: 10 -> 9, of which waited for: 7 -> 5; matrix products, arithmetic and copies ran while one was open for 27% -> 6% of each run, Pallas kernels for 0% -> 31%
where the time goes in v1:
time: 314 us; the launch traced here: 313 us
  waiting for transfers between devices  108 us (34%)
  Pallas kernels  107 us (34%)
  matrix products  21 us (7%)
  starting transfers between devices  19.8 us (6%)
  blocking collectives  15.2 us (5%)
  other arithmetic  14.5 us (5%)
  local copies, waits for them, and re-layouts  14 us (4%)
  between operations  13.7 us (4%)
    all_gather x1, waiting for transfers between devices, local(): pieces = lax.all_gather(pieces, 'band', axis=0, tiled=True)  65.4 us
    pallas_call x1, Pallas kernels, local(): pl.pallas_call(functools.partial(forecast_kernel, lon, strip), grid=(slab...  54.1 us
    pallas_call x1, Pallas kernels, local(): pl.pallas_call(inverse_kernel, out_shape=jax.ShapeDtypeStruct(innovation....  42.3 us
    all_to_all x1, waiting for transfers between devices, local(): lax.all_to_all(pieces, 'col', 0, 0, tiled=True).reshape(obs_total, slab)  22.4 us
    ppermute x3, waiting for transfers between devices, local(): lax.ppermute(x, axis, [(i + 1, i) for i in range(n - 1)])  18.9 us
    all_gather x1, blocking collectives, local(): innovation = lax.all_gather(own_block, 'col', axis=0, tiled=True)  15.2 us
    dot_general x1, matrix products, local(): lax.dot_general(gain, band_rows, (((0,), (0,)), ((), ())), precision=lax....  14.2 us
    ppermute x3, starting transfers between devices, local(): lax.ppermute(x, axis, [(i, i + 1) for i in range(n - 1)])  11.2 us
  transfers between devices with their start and end apart: 9, of which 5 were waited for; matrix products, arithmetic and copies ran while one was open for 6% of the time, Pallas kernels for 31%

profile of v1, /device:TPU:0, one launch (start us, length us, event | category | flops | bytes accessed | tf_op | source)
XLA Modules:
  0.0 313.5 jit_solution(15801969193712813862)
XLA Ops:
  6.5 3.4 %fusion.15 = (f32[1280,256]{1,0:T(8,128)}, f32[1280,256]{1,0:T(8,128)}) fusion(f32[1280,2560]{1,0:T(8,128)} %rest_0_.3), kind=kLoop, calls=%fused_computation.47 | loop fusion | bytes 5242880 | tf_op jit(solution)/shard_map/slice | solution.py:207
  9.9 1.3 collective-permute-start.1
  11.2 5.7 %collective-permute-start = (f32[1280,256]{1,0:T(8,128)}, f32[1280,256]{1,0:T(8,128)S(1)}, u32[]{:S(2)}, u32[]{:S(2)}) collective-permute-start(f32[1280,256]{1,0:T(8,128)} %get-tuple-element.8), channel_id=1, source_target_pairs={{0,8},{8,16},{16,24},{1,9},{9,17},{17,25},{2,10},{10,18},{18,26},{... | collective-permute-start | bytes 3932168 | tf_op jit(solution)/shard_map/ppermute | solution.py:204
  16.9 3.9 %fusion.14 = (f32[160,2560]{1,0:T(8,128)}, f32[160,2560]{1,0:T(8,128)}) fusion(f32[1280,2560]{1,0:T(8,128)} %rest_0_.3), kind=kLoop, calls=%fused_computation.46 | loop fusion | bytes 6553600 | tf_op jit(solution)/shard_map/slice | solution.py:209
  20.8 1.4 collective-permute-start.3
  22.2 4.2 %collective-permute-start.2 = (f32[160,2560]{1,0:T(8,128)}, f32[160,2560]{1,0:T(8,128)}, u32[]{:S(2)}, u32[]{:S(2)}) collective-permute-start(f32[160,2560]{1,0:T(8,128)} %get-tuple-element.6), channel_id=1, source_target_pairs={{0,1},{1,2},{2,3},{3,4},{4,5},{5,6},{6,7},{8,9},{9,10},{10,11},{11... | collective-permute-start | bytes 4915208 | tf_op jit(solution)/shard_map/ppermute | solution.py:204
  27.7 0.7 reshape_reshape.3.row_weights
  28.6 15.9 %collective-permute-done.1.rest_2_ = f32[1280,256]{1,0:T(8,128)S(1)} collective-permute-done((f32[1280,256]{1,0:T(8,128)}, f32[1280,256]{1,0:T(8,128)S(1)}, u32[]{:S(2)}, u32[]{:S(2)}) %collective-permute-start.1) | collective-permute-done | bytes 1310752 | tf_op jit(solution)/shard_map/ppermute | solution.py:205
  44.6 0.6 collective-permute-done.rest_1_
  45.2 0.9 pad_maximum_fusion
  46.1 1.3 collective-permute-start.4
  47.4 0.8 pad_maximum_fusion.1
  48.1 1.3 collective-permute-start.5
  49.6 0.7 dynamic_slice.11.spots
  50.3 0.8 stack.52.lanes
  51.0 2.9 collective-permute-done.5.rest_6_
  54.0 0.7 copy-done.3
  54.7 11.0 %shard_map.65 = f32[48,2560]{1,0:T(8,128)} custom-call(s32[48]{0:T(128)} %dynamic_slice.11.spots, f32[6400]{0:T(1024)} %reshape_reshape.3.row_weights, f32[8,3072]{1,0:T(8,128)} %stack.52.lanes, f32[1280,2560]{1,0:T(8,128)} %rest_0_.3, f32[1280,256]{1,0:T(8,128)} %copy-done.1, f32[1280,256]{1,0:T(8,128)} %copy-done, ...), custom_call_target="tpu_custom_call" | custom-call | flops 10000000 | bytes 13107200 | tf_op jit(solution)/shard_map/pallas_call | solution.py:237
  65.7 1.8 copy.20
  67.6 0.7 all-gather.5.cloned.1.call-update
  68.3 65.4 %all-gather.3.cloned.1.call-done = f32[8,48,1280]{2,1,0:T(8,128)} async-done(((f32[2,48,1280]{2,1,0:T(8,128)}), f32[8,48,1280]{2,1,0:T(8,128)}) %all-gather.3.cloned.1.call-update) | async-done | bytes 1966096 | tf_op jit(solution)/shard_map/all_gather | solution.py:260
  133.7 4.6 %all-to-all-start = ((f32[8,48,1280]{2,1,0:T(8,128)}), f32[8,48,1280]{2,1,0:T(8,128)S(1)}, u32[]{:S(2)}, u32[]{:S(2)}) async-start(f32[8,48,1280]{2,1,0:T(8,128)} %all-gather.3.cloned.1.call-done), calls=%async_computation | async-start | bytes 3932160 | tf_op jit(solution)/shard_map/all_to_all | solution.py:261
  138.7 0.9 pad_bitcast_fusion.row_weights
  139.6 54.1 %shard_map.64 = f32[1280,2560]{1,0:T(8,128)} custom-call(f32[1280,8]{1,0:T(8,128)} %pad_bitcast_fusion.row_weights, f32[8,3072]{1,0:T(8,128)} %stack.52.lanes, f32[1280,2560]{1,0:T(8,128)} %rest_0_.3, f32[1280,256]{1,0:T(8,128)} %copy-done.1, f32[1280,256]{1,0:T(8,128)} %copy-done, f32[160,2560]{1,0:T(8,128)} %collective-permute-done.2.rest_3_, ...), custom_call_target="tpu_custom_call" | custom-call | flops 98304000 | bytes 104857600 | tf_op jit(solution)/shard_map/pallas_call | solution.py:247
  193.8 22.4 %all-to-all-done = f32[8,48,1280]{2,1,0:T(8,128)S(1)} async-done(((f32[8,48,1280]{2,1,0:T(8,128)}), f32[8,48,1280]{2,1,0:T(8,128)S(1)}, u32[]{:S(2)}, u32[]{:S(2)}) %all-to-all-start) | async-done | bytes 1966112 | tf_op jit(solution)/shard_map/all_to_all | solution.py:261
  216.2 1.1 fusion.1
  217.3 15.2 %all_gather.10 = f32[384,384]{1,0:T(8,128)S(1)} all-gather(f32[48,384]{1,0:T(8,128)S(1)} %fusion.1), channel_id=1, replica_groups=mesh['band'=4,'col'=8] {'col'}, dimensions={0}, use_global_device_ids=true | all-gather | bytes 663552 | tf_op jit(solution)/shard_map/all_gather | solution.py:264
  232.5 0.9 add_select_fusion.source
  233.4 42.3 %shard_map.66 = f32[384,384]{1,0:T(8,128)} custom-call(f32[384,384]{1,0:T(8,128)} %add_select_fusion.source), custom_call_target="tpu_custom_call" | custom-call | tf_op jit(solution)/shard_map/pallas_call | solution.py:267
  275.7 5.6 %fusion.18 = f32[384,1280]{1,0:T(8,128)} fusion(f32[384,384]{1,0:T(8,128)} %shard_map.66, f32[384,1280]{1,0:T(8,128)S(1)} %bitcast.43), kind=kOutput, calls=%fused_computation.50 | convolution fusion | flops 2264924160 | bytes 4521984 | tf_op jit(solution)/shard_map/dot_general | solution.py:275
  281.4 14.2 %fusion.19 = f32[1280,2560]{1,0:T(8,128)S(1)} fusion(f32[384,1280]{1,0:T(8,128)} %fusion.18, f32[384,2560]{1,0:T(8,128)} %all-gather.5.cloned.1.call-done), kind=kOutput, calls=%fused_computation.51 | convolution fusion | flops 7549747200 | bytes 19005440 | tf_op jit(solution)/shard_map/dot_general | solution.py:276
  295.6 11.1 %sub.23 = f32[1280,2560]{1,0:T(8,128)} subtract(f32[1280,2560]{1,0:T(8,128)} %shard_map.64, f32[1280,2560]{1,0:T(8,128)S(1)} %fusion.19) | non-fusion elementwise | flops 3276800 | bytes 39321600 | tf_op jit(solution)/shard_map/sub | solution.py:277
  (59 shorter events, 2.1 us)
Async XLA Ops:
  6.5 127.2 %all-gather.3.cloned.1.call-start = ((), (), s32[]{:S(2)}) async-start(), calls=%async_computation.1 | async-start | bytes 2457600 | tf_op jit(solution)/shard_map/all_gather | solution.py:260
  9.9 34.6 %collective-permute-start.1 = (f32[1280,256]{1,0:T(8,128)}, f32[1280,256]{1,0:T(8,128)S(1)}, u32[]{:S(2)}, u32[]{:S(2)}) collective-permute-start(f32[1280,256]{1,0:T(8,128)} %get-tuple-element.7), channel_id=1, source_target_pairs={{8,0},{16,8},{24,16},{9,1},{17,9},{25,17},{10,2},{18,10},{26,18},{... | collective-permute-start | bytes 3932168 | tf_op jit(solution)/shard_map/ppermute | solution.py:205
  11.2 15.3 %copy-start.5 = (f32[64,160]{1,0:T(8,128)S(1)}, f32[64,160]{1,0:T(8,128)}, u32[]{:S(2)}) copy-start(f32[64,160]{1,0:T(8,128)} %param.7) | copy-start | bytes 122884
  11.2 15.3 %copy-start.4 = (f32[64,160]{1,0:T(8,128)S(1)}, f32[64,160]{1,0:T(8,128)}, u32[]{:S(2)}) copy-start(f32[64,160]{1,0:T(8,128)} %param.8) | copy-start | bytes 122884
  11.2 15.3 %copy-start.7 = (pred[64]{0:T(512)(128)(4,1)S(1)}, pred[64]{0:T(512)(128)(4,1)}, u32[]{:S(2)}) copy-start(pred[64]{0:T(512)(128)(4,1)} %constant.15.clone.1) | copy-start | bytes 196
  11.2 33.9 %collective-permute-start = (f32[1280,256]{1,0:T(8,128)}, f32[1280,256]{1,0:T(8,128)S(1)}, u32[]{:S(2)}, u32[]{:S(2)}) collective-permute-start(f32[1280,256]{1,0:T(8,128)} %get-tuple-element.8), channel_id=1, source_target_pairs={{0,8},{8,16},{16,24},{1,9},{9,17},{17,25},{2,10},{10,18},{18,26},{... | collective-permute-start | bytes 3932168 | tf_op jit(solution)/shard_map/ppermute | solution.py:204
  20.8 7.6 %copy-start.6 = (s32[3,128]{1,0:T(4,128)S(1)}, s32[3,128]{1,0:T(4,128)}, u32[]{:S(2)}) copy-start(s32[3,128]{1,0:T(4,128)} %param.9) | copy-start | bytes 4612
  20.8 33.2 %collective-permute-start.3 = (f32[160,2560]{1,0:T(8,128)}, f32[160,2560]{1,0:T(8,128)}, u32[]{:S(2)}, u32[]{:S(2)}) collective-permute-start(f32[160,2560]{1,0:T(8,128)} %get-tuple-element.5), channel_id=1, source_target_pairs={{1,0},{2,1},{3,2},{4,3},{5,4},{6,5},{7,6},{9,8},{10,9},{11,10},{12... | collective-permute-start | bytes 4915208 | tf_op jit(solution)/shard_map/ppermute | solution.py:205
  22.2 31.8 %collective-permute-start.2 = (f32[160,2560]{1,0:T(8,128)}, f32[160,2560]{1,0:T(8,128)}, u32[]{:S(2)}, u32[]{:S(2)}) collective-permute-start(f32[160,2560]{1,0:T(8,128)} %get-tuple-element.6), channel_id=1, source_target_pairs={{0,1},{1,2},{2,3},{3,4},{4,5},{5,6},{6,7},{8,9},{9,10},{10,11},{11... | collective-permute-start | bytes 4915208 | tf_op jit(solution)/shard_map/ppermute | solution.py:204
  26.7 22.8 %copy-start.9 = (s32[3,128]{1,0:T(4,128)S(1)}, s32[3,128]{1,0:T(4,128)}, u32[]{:S(2)}) copy-start(s32[3,128]{1,0:T(4,128)} %param.10) | copy-start | bytes 4612
  44.5 9.5 %copy-start = (f32[1280,256]{1,0:T(8,128)}, f32[1280,256]{1,0:T(8,128)S(1)}, u32[]{:S(2)}) copy-start(f32[1280,256]{1,0:T(8,128)S(1)} %collective-permute-done.1.rest_2_) | copy-start | bytes 3932164
  45.2 8.8 %copy-start.1 = (f32[1280,256]{1,0:T(8,128)}, f32[1280,256]{1,0:T(8,128)S(1)}, u32[]{:S(2)}) copy-start(f32[1280,256]{1,0:T(8,128)S(1)} %collective-permute-done.rest_1_) | copy-start | bytes 3932164
  46.1 5.0 %collective-permute-start.4 = (f32[160,512]{1,0:T(8,128)}, f32[160,512]{1,0:T(8,128)S(1)}, u32[]{:S(2)}, u32[]{:S(2)}) collective-permute-start(f32[160,512]{1,0:T(8,128)} %pad_maximum_fusion), channel_id=1, source_target_pairs={{0,1},{1,2},{2,3},{3,4},{4,5},{5,6},{6,7},{8,9},{9,10},{10,11},{11... | collective-permute-start | bytes 983048 | tf_op jit(solution)/shard_map/ppermute | solution.py:204
  48.1 5.8 %collective-permute-start.5 = (f32[160,512]{1,0:T(8,128)}, f32[160,512]{1,0:T(8,128)S(1)}, u32[]{:S(2)}, u32[]{:S(2)}) collective-permute-start(f32[160,512]{1,0:T(8,128)} %pad_maximum_fusion.1), channel_id=1, source_target_pairs={{1,0},{2,1},{3,2},{4,3},{5,4},{6,5},{7,6},{9,8},{10,9},{11,10},{12... | collective-permute-start | bytes 983048 | tf_op jit(solution)/shard_map/ppermute | solution.py:205
  51.0 3.0 copy-start.2
  54.0 0.7 copy-start.3
  67.6 213.8 %all-gather.5.cloned.1.call-start = ((), (), s32[]{:S(2)}) async-start(), calls=%async_computation.2 | async-start | bytes 4423680 | tf_op jit(solution)/shard_map/all_gather | solution.py:258
  68.3 70.3 %copy-start.10 = (f32[3,128]{1,0:T(4,128)S(1)}, f32[3,128]{1,0:T(4,128)}, u32[]{:S(2)}) copy-start(f32[3,128]{1,0:T(4,128)} %param.11) | copy-start | bytes 4612
  133.7 82.5 %all-to-all-start = ((f32[8,48,1280]{2,1,0:T(8,128)}), f32[8,48,1280]{2,1,0:T(8,128)S(1)}, u32[]{:S(2)}, u32[]{:S(2)}) async-start(f32[8,48,1280]{2,1,0:T(8,128)} %all-gather.3.cloned.1.call-done), calls=%async_computation | async-start | bytes 3932160 | tf_op jit(solution)/shard_map/all_to_all | solution.py:261
  139.6 76.5 %copy-start.8 = (s32[48]{0:T(128)S(1)}, s32[48]{0:T(128)}, u32[]{:S(2)}) copy-start(s32[48]{0:T(128)} %dynamic_slice.11.spots) | copy-start | bytes 580
Sparse Core Ops, SparseCore 0:
  67.7 65.9 all-gather.2
  135.3 79.6 all-gather.4
